TPU v7x, 512 devices: a whole 4x4x16 slice. The times are simulated.
512 devices in a mesh: sub: 64 (over z, x), beam: 8 (over y, core).
Axes of the slice: x: 4, y: 4, z: 16, core: 2. Of those that a mesh axis runs over, the one named last changes fastest.
Arguments:
- intensity: float32 [16, 8192, 256], P(None, ('sub', 'beam')), may hold values from -6 to 6
- shift_table: int32 [11, 2048], replicated, may hold values from 0 to 154, as said below
- box_widths: int32 [8], replicated, may hold values from 1 to 64, as said below
Outputs:
- dm_plane: float32 [16, 2048, 256], P('beam', 'sub')
- peaks: float32 [16, 16, 2048], P('beam', None, 'sub')
Inputs may be any that keep to these rules, and one draw needn't show every extreme that they name: `shift_table`: entry (l, d) is the delay in samples given to the upper half at level l + 1 for DM row d; it rises with d up to a dither of one sample, and entries with d at or over 2^(l + 1) are not read. `box_widths`: 8 different widths; 1 and 64 are always among them.
All inputs are finite; a program needn't handle non-finite values.
Results may differ from a plain program's by a relative error of at most 0.00013.
Values sent between devices are 32-bit elements; how exact they have to be, the bound alone decides.
No kernel may reach another device: no remote copies, remote signals or barrier semaphores. Data moves between devices by JAX's collectives and lax.ppermute only.
A program may use at most 64 MiB of HBM per device.

v0:
```python
import jax
import jax.numpy as jnp
from jax import lax
from jax.sharding import PartitionSpec as P

GROUP = 4
GTAPS = 64


def swapped(block, axis, distance):
    count = lax.axis_size(axis)
    route = []
    for low in range(count):
        high = low | 1 << distance
        if high != low and high < count:
            route += [(low, high), (high, low)]
    return lax.ppermute(block, axis, route)


def shift_rows(series, delays):
    length = series.shape[-1]
    result = series
    amounts = delays[:, None]
    for place in range(length.bit_length()):
        step = 1 << place
        if step >= length:
            moved = jnp.zeros_like(result)
        else:
            filler = jnp.zeros(result.shape[:-1] + (step,), result.dtype)
            moved = jnp.concatenate([result[..., step:], filler], axis=-1)
        taken = amounts >> place & 1 == 1
        result = jnp.where(taken, moved, result)
    return result


def merge_halves(lower, upper, delays):
    return jnp.repeat(lower, 2, axis=-2) + shift_rows(jnp.repeat(upper, 2, axis=-2), delays)


def box_peaks(plane, widths):
    length = plane.shape[-1]
    prefix = jnp.concatenate(
        [jnp.zeros(plane.shape[:-1] + (1,), plane.dtype), jnp.cumsum(plane, axis=-1)], axis=-1
    )
    tail = jnp.broadcast_to(prefix[..., -1:], plane.shape[:-1] + (GTAPS,))
    padded = jnp.concatenate([prefix, tail], axis=-1)

    def single(width):
        ahead = lax.dynamic_slice_in_dim(padded, width, length, axis=padded.ndim - 1)
        return jnp.max(ahead - prefix[..., :length], axis=-1) / jnp.sqrt(width.astype(plane.dtype))

    return jax.vmap(single)(widths)


def gauss_peaks(plane, widths):
    beams_dev, rows, length = plane.shape
    taps = jnp.arange(GTAPS, dtype=jnp.float32)
    sigma = widths.astype(jnp.float32) / 2.3548
    center = float(GTAPS // 2)
    shape = jnp.exp(-0.5 * ((taps[None, :] - center) / sigma[:, None]) ** 2)
    norm = jnp.sqrt(jnp.sum(shape * shape, axis=1))
    lag = jnp.arange(256, dtype=jnp.int32)[:, None] - jnp.arange(128, dtype=jnp.int32)[None, :]
    valid = (lag >= 0) & (lag < GTAPS)
    offset = lag.astype(jnp.float32)[None, :, :] - center
    kernel = jnp.exp(-0.5 * (offset / sigma[:, None, None]) ** 2) / norm[:, None, None]
    kernel = jnp.where(valid[None], kernel, jnp.zeros_like(kernel))
    pieces = plane.reshape(beams_dev, rows, length // 128, 128)
    following = jnp.concatenate([pieces[:, :, 1:], jnp.zeros_like(pieces[:, :, :1])], axis=2)
    window = jnp.concatenate([pieces, following], axis=3)
    filtered = jnp.einsum("brnj,wjo->wbrno", window, kernel, precision=lax.Precision.HIGHEST)
    return jnp.max(filtered, axis=(3, 4))


def on_device(intensity, shift_table, box_widths):
    beams_all, chan_dev, length = intensity.shape
    sub_count = lax.axis_size("sub")
    beam_count = lax.axis_size("beam")
    scale = float(chan_dev * sub_count * beam_count) ** (-0.5)
    turned = lax.all_to_all(intensity, "beam", split_axis=0, concat_axis=1, tiled=True)
    rows = (
        jnp.sum(turned.reshape(turned.shape[0], turned.shape[1] // GROUP, GROUP, length), axis=2)
        * scale
    )
    beams_dev, block_rows, _ = rows.shape
    size = 1
    level = 0
    while size < block_rows:
        grouped = rows.reshape(beams_dev, block_rows // (2 * size), 2, size, length)
        merged = merge_halves(grouped[:, :, 0], grouped[:, :, 1], shift_table[level, : 2 * size])
        rows = merged.reshape(beams_dev, block_rows, length)
        size = size * 2
        level = level + 1
    place = lax.axis_index("sub")
    nbits = sub_count.bit_length() - 1
    block = jnp.zeros((), jnp.int32)
    half = block_rows // 2
    for bit in range(nbits):
        upper_side = place >> bit & 1
        first = rows[:, :half]
        second = rows[:, half:]
        outgoing = jnp.where(upper_side == 1, first, second)
        kept = jnp.where(upper_side == 1, second, first)
        arrived = swapped(outgoing, "sub", bit)
        lower = jnp.where(upper_side == 1, arrived, kept)
        upper = jnp.where(upper_side == 1, kept, arrived)
        block = 2 * block + upper_side
        delays = lax.dynamic_slice_in_dim(shift_table[level], block * block_rows, block_rows)
        rows = merge_halves(lower, upper, delays)
        level = level + 1
    boxed = jnp.transpose(box_peaks(rows, box_widths), (1, 0, 2))
    gaussed = jnp.transpose(gauss_peaks(rows, box_widths), (1, 0, 2))
    return (rows, jnp.concatenate([boxed, gaussed], axis=1))


def solution(mesh):
    in_specs = (P(None, ("sub", "beam"), None), P(), P())
    out_specs = (P("beam", "sub", None), P("beam", None, "sub"))
    return jax.shard_map(
        on_device, mesh=mesh, in_specs=in_specs, out_specs=out_specs, check_vma=False
    )
```

profile of v0, /device:TPU:8, one launch (start us, length us, event | category | flops | bytes accessed | tf_op | source)
XLA Modules:
  0.0 91.2 jit_solution(8298401645639579027)
XLA Ops:
  0.6 9.2 %all-to-all-start = ((f32[16,16,256]{2,1,0:T(8,128)}), f32[16,16,256]{2,1,0:T(8,128)S(1)}, u32[]{:S(2)}, u32[]{:S(2)}) async-start(f32[16,16,256]{2,1,0:T(8,128)} %param.3), calls=%async_computation | async-start | bytes 524288 | tf_op jit(solution)/shard_map/all_to_all | solution.py:79
  9.8 0.7 compare_bitcast_fusion.98
  10.5 0.7 compare_bitcast_fusion.89
  11.2 0.7 compare_bitcast_fusion.80
  11.9 0.7 compare_bitcast_fusion.71
  12.6 0.7 compare_bitcast_fusion.62
  13.3 1.0 %fusion.31 = (s32[1,2048]{1,0:T(1,128)S(1)}, s32[1,2048]{1,0:T(1,128)S(1)}, s32[1,2048]{1,0:T(1,128)S(1)}, s32[1,2048]{1,0:T(1,128)S(1)}, s32[1,2048]{1,0:T(1,128)S(1)}, /*index=5*/s32[1,2048]{1,0:T(1,128)S(1)}) fusion(s32[11,2048]{1,0:T(8,128)} %param.4), kind=kLoop, calls=%fused_computation.279 | loop fusion | bytes 98304 | tf_op jit(solution)/shard_map/slice | solution.py:107
  14.9 1.0 %all-to-all-done = f32[16,16,256]{2,1,0:T(8,128)S(1)} async-done(((f32[16,16,256]{2,1,0:T(8,128)}), f32[16,16,256]{2,1,0:T(8,128)S(1)}, u32[]{:S(2)}, u32[]{:S(2)}) %all-to-all-start) | async-done | bytes 262176 | tf_op jit(solution)/shard_map/all_to_all | solution.py:79
  15.9 0.2 copy.57
  16.1 0.1 reduce_sum.18
  16.4 0.1 pad_select_fusion.76
  16.5 0.1 slice.511
  16.7 0.1 pad_select_fusion.75
  16.8 0.1 slice.512
  16.9 0.1 pad_select_fusion.74
  17.0 0.1 slice.513
  17.2 0.1 pad_select_fusion.73
  17.3 0.1 slice.514
  17.4 0.1 pad_select_fusion.72
  17.5 0.1 slice.515
  17.7 0.1 pad_select_fusion.71
  17.8 0.1 slice.516
  17.9 0.1 pad_select_fusion.70
  18.0 0.1 select_add_fusion.8
  19.7 0.1 select_add_fusion.7
  24.2 1.9 %collective-permute-start = (f32[2,16,256]{2,1,0:T(8,128)S(1)}, f32[2,16,256]{2,1,0:T(8,128)S(1)}, u32[]{:S(2)}, u32[]{:S(2)}) collective-permute-start(f32[2,16,256]{2,1,0:T(8,128)S(1)} %slice_select_fusion.11), channel_id=1, source_target_pairs={{0,8},{8,0},{16,24},{24,16},{32,40},{40,32},{48,56},{56,48},{64,72... | collective-permute-start | bytes 98312 | tf_op jit(solution)/shard_map/ppermute | solution.py:17
  26.1 3.9 %collective-permute-done = f32[2,16,256]{2,1,0:T(8,128)S(1)} collective-permute-done((f32[2,16,256]{2,1,0:T(8,128)S(1)}, f32[2,16,256]{2,1,0:T(8,128)S(1)}, u32[]{:S(2)}, u32[]{:S(2)}) %collective-permute-start) | collective-permute-done | bytes 32800 | tf_op jit(solution)/shard_map/ppermute | solution.py:17
  31.5 1.9 %collective-permute-start.1 = (f32[2,16,256]{2,1,0:T(8,128)S(1)}, f32[2,16,256]{2,1,0:T(8,128)S(1)}, u32[]{:S(2)}, u32[]{:S(2)}) collective-permute-start(f32[2,16,256]{2,1,0:T(8,128)S(1)} %slice_select_fusion.9), channel_id=1, source_target_pairs={{0,16},{16,0},{8,24},{24,8},{32,48},{48,32},{40,56},{56,40},{64,80... | collective-permute-start | bytes 98312 | tf_op jit(solution)/shard_map/ppermute | solution.py:17
  33.4 5.4 %collective-permute-done.1 = f32[2,16,256]{2,1,0:T(8,128)S(1)} collective-permute-done((f32[2,16,256]{2,1,0:T(8,128)S(1)}, f32[2,16,256]{2,1,0:T(8,128)S(1)}, u32[]{:S(2)}, u32[]{:S(2)}) %collective-permute-start.1) | collective-permute-done | bytes 32800 | tf_op jit(solution)/shard_map/ppermute | solution.py:17
  40.3 1.9 %collective-permute-start.2 = (f32[2,16,256]{2,1,0:T(8,128)S(1)}, f32[2,16,256]{2,1,0:T(8,128)S(1)}, u32[]{:S(2)}, u32[]{:S(2)}) collective-permute-start(f32[2,16,256]{2,1,0:T(8,128)S(1)} %slice_select_fusion.7), channel_id=1, source_target_pairs={{0,32},{32,0},{8,40},{40,8},{16,48},{48,16},{24,56},{56,24},{64,96... | collective-permute-start | bytes 98312 | tf_op jit(solution)/shard_map/ppermute | solution.py:17
  42.2 3.9 %collective-permute-done.2 = f32[2,16,256]{2,1,0:T(8,128)S(1)} collective-permute-done((f32[2,16,256]{2,1,0:T(8,128)S(1)}, f32[2,16,256]{2,1,0:T(8,128)S(1)}, u32[]{:S(2)}, u32[]{:S(2)}) %collective-permute-start.2) | collective-permute-done | bytes 32800 | tf_op jit(solution)/shard_map/ppermute | solution.py:17
  47.5 1.9 %collective-permute-start.3 = (f32[2,16,256]{2,1,0:T(8,128)S(1)}, f32[2,16,256]{2,1,0:T(8,128)S(1)}, u32[]{:S(2)}, u32[]{:S(2)}) collective-permute-start(f32[2,16,256]{2,1,0:T(8,128)S(1)} %slice_select_fusion.5), channel_id=1, source_target_pairs={{0,64},{64,0},{8,72},{72,8},{16,80},{80,16},{24,88},{88,24},{32,96... | collective-permute-start | bytes 98312 | tf_op jit(solution)/shard_map/ppermute | solution.py:17
  49.5 4.8 %collective-permute-done.3 = f32[2,16,256]{2,1,0:T(8,128)S(1)} collective-permute-done((f32[2,16,256]{2,1,0:T(8,128)S(1)}, f32[2,16,256]{2,1,0:T(8,128)S(1)}, u32[]{:S(2)}, u32[]{:S(2)}) %collective-permute-start.3) | collective-permute-done | bytes 32800 | tf_op jit(solution)/shard_map/ppermute | solution.py:17
  55.7 5.2 %collective-permute-start.4 = (f32[2,16,256]{2,1,0:T(8,128)S(1)}, f32[2,16,256]{2,1,0:T(8,128)S(1)}, u32[]{:S(2)}, u32[]{:S(2)}) collective-permute-start(f32[2,16,256]{2,1,0:T(8,128)S(1)} %slice_select_fusion.3), channel_id=1, source_target_pairs={{0,128},{128,0},{8,136},{136,8},{16,144},{144,16},{24,152},{152,24... | collective-permute-start | bytes 98312 | tf_op jit(solution)/shard_map/ppermute | solution.py:17
  60.9 0.2 fusion.24
  61.1 4.5 %collective-permute-done.4 = f32[2,16,256]{2,1,0:T(8,128)S(1)} collective-permute-done((f32[2,16,256]{2,1,0:T(8,128)S(1)}, f32[2,16,256]{2,1,0:T(8,128)S(1)}, u32[]{:S(2)}, u32[]{:S(2)}) %collective-permute-start.4) | collective-permute-done | bytes 32800 | tf_op jit(solution)/shard_map/ppermute | solution.py:17
  67.1 11.5 %collective-permute-start.5 = (f32[2,16,256]{2,1,0:T(8,128)S(1)}, f32[2,16,256]{2,1,0:T(8,128)S(1)}, u32[]{:S(2)}, u32[]{:S(2)}) collective-permute-start(f32[2,16,256]{2,1,0:T(8,128)S(1)} %slice_select_fusion.1), channel_id=1, source_target_pairs={{0,256},{256,0},{8,264},{264,8},{16,272},{272,16},{24,280},{280,24... | collective-permute-start | bytes 98312 | tf_op jit(solution)/shard_map/ppermute | solution.py:17
  78.7 3.0 %collective-permute-done.5 = f32[2,16,256]{2,1,0:T(8,128)S(1)} collective-permute-done((f32[2,16,256]{2,1,0:T(8,128)S(1)}, f32[2,16,256]{2,1,0:T(8,128)S(1)}, u32[]{:S(2)}, u32[]{:S(2)}) %collective-permute-start.5) | collective-permute-done | bytes 32800 | tf_op jit(solution)/shard_map/ppermute | solution.py:17
  83.1 1.2 %reduce-window.6 = f32[2,32,2,128]{3,1,2,0:T(8,128)S(1)} reduce-window(f32[2,32,2,128]{3,1,2,0:T(8,128)S(1)} %copy_bitcast_fusion.1, f32[]{:T(128)} %constant.29.clone.1), window={size=1x1x1x128 pad=0_0x0_0x0_0x127_0}, to_apply=%region_1.2 | reduce-window | flops 2080768 | bytes 131076 | tf_op jit(solution)/shard_map/reduce-window
  84.3 0.2 slice_reduce_fusion
  84.6 0.2 slice_reduce_fusion.1
  84.9 0.1 pad_maximum_fusion
  85.0 0.2 copy.65
  85.2 0.2 copy.66
  85.4 2.8 %gather_fusion = f32[8,2,32,256]{2,1,3,0:T(2,128)S(1)} fusion(f32[2,32,321]{1,0,2:T(2,128)S(1)} %copy.65, s32[8]{0:T(128)S(1)} %fusion.26), kind=kCustom, calls=%fused_computation | custom fusion | bytes 1048672 | tf_op jit(solution)/shard_map/vmap()/gather | solution.py:49
  88.2 1.1 %subtract_reduce_fusion = f32[8,2,32]{2,1,0:T(2,128)S(1)} fusion(f32[8,2,32,256]{2,1,3,0:T(2,128)S(1)} %gather_fusion, f32[2,32,256]{1,0,2:T(2,128)S(1)} %copy.66), kind=kLoop, calls=%fused_computation.1 | loop fusion | flops 261632 | bytes 591872 | tf_op jit(solution)/shard_map/vmap()/reduce_max | solution.py:50
  89.4 1.1 %convolution_reduce_fusion = f32[8,2,32]{2,1,0:T(2,128)S(1)} fusion(f32[8]{0:T(128)S(1)} %sqrt.11, f32[8]{0:T(128)S(1)} %get-tuple-element.92, f32[256,128]{1,0:T(8,128)S(1)} %convert_add_fusion, pred[256,128]{1,0:T(8,128)(4,1)S(1)} %fusion.18, f32[2,32,1,128]{3,1,2,0:T(8,128)S(1)} %slice.621, f32[2,32,2,128]{3,1,2,0:T(8,128)S(1)} %copy_bitcast_fusion.1), kind=kOutput, calls=%fused_computation.2 | convolution fusion | flops 404192768 | bytes 264256 | tf_op jit(solution)/shard_map/brnj,wjo->wbrno/dot_general | solution.py:70
  90.6 0.6 copy.69
  (254 shorter events, 15.3 us)
Async XLA Ops:
  0.6 15.3 %all-to-all-start = ((f32[16,16,256]{2,1,0:T(8,128)}), f32[16,16,256]{2,1,0:T(8,128)S(1)}, u32[]{:S(2)}, u32[]{:S(2)}) async-start(f32[16,16,256]{2,1,0:T(8,128)} %param.3), calls=%async_computation | async-start | bytes 524288 | tf_op jit(solution)/shard_map/all_to_all | solution.py:79
  22.3 3.8 %copy-start.1 = (s32[8]{0:T(128)S(1)}, s32[8]{0:T(128)}, u32[]{:S(2)}) copy-start(s32[8]{0:T(128)} %param.5) | copy-start | bytes 100
  24.2 5.8 %collective-permute-start = (f32[2,16,256]{2,1,0:T(8,128)S(1)}, f32[2,16,256]{2,1,0:T(8,128)S(1)}, u32[]{:S(2)}, u32[]{:S(2)}) collective-permute-start(f32[2,16,256]{2,1,0:T(8,128)S(1)} %slice_select_fusion.11), channel_id=1, source_target_pairs={{0,8},{8,0},{16,24},{24,16},{32,40},{40,32},{48,56},{56,48},{64,72... | collective-permute-start | bytes 98312 | tf_op jit(solution)/shard_map/ppermute | solution.py:17
  31.5 7.3 %collective-permute-start.1 = (f32[2,16,256]{2,1,0:T(8,128)S(1)}, f32[2,16,256]{2,1,0:T(8,128)S(1)}, u32[]{:S(2)}, u32[]{:S(2)}) collective-permute-start(f32[2,16,256]{2,1,0:T(8,128)S(1)} %slice_select_fusion.9), channel_id=1, source_target_pairs={{0,16},{16,0},{8,24},{24,8},{32,48},{48,32},{40,56},{56,40},{64,80... | collective-permute-start | bytes 98312 | tf_op jit(solution)/shard_map/ppermute | solution.py:17
  40.3 5.8 %collective-permute-start.2 = (f32[2,16,256]{2,1,0:T(8,128)S(1)}, f32[2,16,256]{2,1,0:T(8,128)S(1)}, u32[]{:S(2)}, u32[]{:S(2)}) collective-permute-start(f32[2,16,256]{2,1,0:T(8,128)S(1)} %slice_select_fusion.7), channel_id=1, source_target_pairs={{0,32},{32,0},{8,40},{40,8},{16,48},{48,16},{24,56},{56,24},{64,96... | collective-permute-start | bytes 98312 | tf_op jit(solution)/shard_map/ppermute | solution.py:17
  47.5 6.7 %collective-permute-start.3 = (f32[2,16,256]{2,1,0:T(8,128)S(1)}, f32[2,16,256]{2,1,0:T(8,128)S(1)}, u32[]{:S(2)}, u32[]{:S(2)}) collective-permute-start(f32[2,16,256]{2,1,0:T(8,128)S(1)} %slice_select_fusion.5), channel_id=1, source_target_pairs={{0,64},{64,0},{8,72},{72,8},{16,80},{80,16},{24,88},{88,24},{32,96... | collective-permute-start | bytes 98312 | tf_op jit(solution)/shard_map/ppermute | solution.py:17
  55.7 9.9 %collective-permute-start.4 = (f32[2,16,256]{2,1,0:T(8,128)S(1)}, f32[2,16,256]{2,1,0:T(8,128)S(1)}, u32[]{:S(2)}, u32[]{:S(2)}) collective-permute-start(f32[2,16,256]{2,1,0:T(8,128)S(1)} %slice_select_fusion.3), channel_id=1, source_target_pairs={{0,128},{128,0},{8,136},{136,8},{16,144},{144,16},{24,152},{152,24... | collective-permute-start | bytes 98312 | tf_op jit(solution)/shard_map/ppermute | solution.py:17
  67.1 14.5 %collective-permute-start.5 = (f32[2,16,256]{2,1,0:T(8,128)S(1)}, f32[2,16,256]{2,1,0:T(8,128)S(1)}, u32[]{:S(2)}, u32[]{:S(2)}) collective-permute-start(f32[2,16,256]{2,1,0:T(8,128)S(1)} %slice_select_fusion.1), channel_id=1, source_target_pairs={{0,256},{256,0},{8,264},{264,8},{16,272},{272,16},{24,280},{280,24... | collective-permute-start | bytes 98312 | tf_op jit(solution)/shard_map/ppermute | solution.py:17
  83.1 6.2 %copy-start = (f32[2,32,256]{2,1,0:T(8,128)}, f32[2,32,256]{2,1,0:T(8,128)S(1)}, u32[]{:S(2)}) copy-start(f32[2,32,256]{2,1,0:T(8,128)S(1)} %select_add_fusion) | copy-start | bytes 196612
where the time goes:
time: 91.7 us; the launch traced here: 91.2 us
  starting transfers between devices  33.5 us (37%)
  waiting for transfers between devices  26.2 us (29%)
  other arithmetic  14.8 us (16%)
  local copies, waits for them, and re-layouts  13.7 us (15%)
  between operations  1.77 us (2%)
  matrix products  1.15 us (1%)
    ppermute x6, waiting for transfers between devices, swapped(): return lax.ppermute(block, axis, route)  25.3 us
    ppermute x6, starting transfers between devices, swapped(): return lax.ppermute(block, axis, route)  24.4 us
    all_to_all x1, starting transfers between devices, on_device(): lax.all_to_all(intensity, 'beam', split_axis=0, concat_axis=1, tiled=True)  9.15 us
    select_n x77, other arithmetic, shift_rows(): result = jnp.where(taken, moved, result)  6.7 us
    slice x89, local copies, waits for them, and re-layouts, shift_rows(): moved = jnp.concatenate([result[..., step:], filler], axis=-1)  6.61 us
    eq x14, other arithmetic, shift_rows(): taken = amounts >> place & 1 == 1  4.04 us
    gather x1, local copies, waits for them, and re-layouts, single(): lax.dynamic_slice_in_dim(padded, width, length, axis=padded.ndim - 1)  2.79 us
  transfers between devices with their start and end apart: 7, of which 7 were waited for; matrix products, arithmetic and copies ran while one was open for 6% of the time, Pallas kernels for 0%

commit v1 on v0

v1 whole, which is shorter than its diff:
```python
import functools

import jax
import jax.numpy as jnp
from jax import lax
from jax.experimental import pallas as pl
from jax.experimental.pallas import tpu as pltpu
from jax.sharding import Mesh, PartitionSpec as P

GTAPS = 64
LANES = 128
F32 = jnp.float32
BF16 = jnp.bfloat16
SMEM = pltpu.SMEM
VMEM = pltpu.VMEM
LANEWISE = lax.GatherDimensionNumbers(
    offset_dims=(),
    collapsed_slice_dims=(1,),
    start_index_map=(1,),
    operand_batching_dims=(0,),
    start_indices_batching_dims=(0,),
)


def pick(block, index):
    return lax.gather(
        block, index[..., None], LANEWISE, (1, 1), mode=lax.GatherScatterMode.PROMISE_IN_BOUNDS
    )


def reversed_bits(value, bits):
    result = 0
    for place in range(bits):
        result = result + (value // (1 << place)) % 2 * (1 << (bits - 1 - place))
    return result


def iota(axis):
    return lax.broadcasted_iota(jnp.int32, (8, LANES), axis)


def delayed_pair(first, second, delay):
    source = iota(1) + delay
    index = source & (LANES - 1)
    near = source < LANES
    a = pick(first, index)
    b = pick(second, index)
    zero = jnp.zeros_like(a)
    return (
        jnp.where(near, a, jnp.where(source < 2 * LANES, b, zero)),
        jnp.where(near, b, zero),
    )


def merge_pair(lower, upper, delay):
    moved = delayed_pair(*upper, delay)
    return lower[0] + moved[0], lower[1] + moved[1]


def first_kernel(scale, table, x, out, split):
    beams = x.shape[0] // 16
    for half in range(2):
        split[half] = x[:, half * LANES : (half + 1) * LANES]
    for tile in range(beams // 8):
        subbands = []
        for s in range(4):
            halves = []
            for half in range(2):
                parts = [
                    split[half, pl.ds(tile * 128 + 4 * s + c, 8, stride=16), :]
                    for c in range(4)
                ]
                halves.append(((parts[0] + parts[1]) + (parts[2] + parts[3])) * scale)
            subbands.append(tuple(halves))
        pairs = [
            [merge_pair(subbands[2 * g], subbands[2 * g + 1], table[0, d]) for d in range(2)]
            for g in range(2)
        ]
        for target in range(4):
            d = (target & 1) * 2 + (target >> 1)
            row = merge_pair(pairs[0][d >> 1], pairs[1][d >> 1], table[1, d])
            for half in range(2):
                for j in range(4):
                    out[target * 8 + tile * 4 + j, 2 * half : 2 * half + 2, :] = row[half][
                        2 * j : 2 * j + 2, :
                    ]


class Delay:
    def __init__(self, low, high):
        lane, sublane = iota(1), iota(0)
        source = lane + jnp.where(sublane < 4, low, high)
        self.index = source & (LANES - 1)
        self.near = source < LANES
        self.next = (source < 2 * LANES) & ((sublane & 2) == 0)

    def __call__(self, block):
        a = pick(block, self.index)
        other = pltpu.roll(a, 6, 0)
        return jnp.where(self.near, a, jnp.where(self.next, other, jnp.zeros_like(a)))


def merge_blocks(blocks, bit, delay_of):
    delays = {}
    merged = [None] * len(blocks)
    for v in range(len(blocks)):
        kind = v & ((2 << bit) - 1)
        if kind not in delays:
            delays[kind] = delay_of(kind)
        merged[v] = blocks[v & ~(1 << bit)] + delays[kind](blocks[v | 1 << bit])
    return merged


def block_row(v, bits):
    return sum((v >> m & 1) << (bits - 1 - m) for m in range(bits))


def second_kernel(table, x, out):
    low = iota(0) < 4
    top = reversed_bits(lax.axis_index("x"), 2)
    delay = Delay(table[2, top * 2], table[2, top * 2 + 1])
    blocks = []
    for v in range(16):
        a = x[v]
        b = pltpu.roll(a, 4, 0)
        blocks.append(jnp.where(low, a, b) + delay(jnp.where(low, b, a)))
    for bit in range(4):
        base = top * (4 << bit)

        def delay_of(v, bit=bit, base=base):
            row = base + block_row(v, bit + 1)
            return Delay(table[bit + 3, row], table[bit + 3, row + (2 << bit)])

        blocks = merge_blocks(blocks, bit, delay_of)
    for w in range(8):
        a, b = blocks[w], blocks[8 + w]
        out[2 * w] = jnp.where(low, a, pltpu.roll(b, 4, 0))
        out[2 * w + 1] = jnp.where(low, pltpu.roll(a, 4, 0), b)


def prepare_kernel(table, widths, delays, box_gauss, gauss_rest):
    block = reversed_bits(lax.axis_index("x"), 2) * 16 + reversed_bits(lax.axis_index("z"), 4)
    for n in range(4):
        base = block * (4 << n)
        row = table[7 + n : 8 + n, pl.ds(pl.multiple_of(base // LANES * LANES, LANES), LANES)]
        delays[n : n + 1, :] = pltpu.roll(row, (LANES - base % LANES) % LANES, 1)
    shape = (GTAPS, LANES)
    lag = lax.broadcasted_iota(jnp.int32, shape, 1) - lax.broadcasted_iota(jnp.int32, shape, 0)
    valid = (lag >= 0) & (lag < GTAPS)
    offset = lag.astype(F32) - float(GTAPS // 2)
    for i in range(8):
        rows = pl.ds(i * GTAPS, GTAPS)
        ones = jnp.where((lag >= 0) & (lag < widths[i]), 1.0, 0.0).astype(BF16)
        box_gauss[rows, 0:LANES] = ones
        box_gauss[rows, LANES : 2 * LANES] = ones
        sigma = jnp.full(shape, widths[i], jnp.int32).astype(F32) / 2.3548
        taps = jnp.where(valid, jnp.exp(-0.5 * (offset / sigma) ** 2), 0.0)
        taps = taps / jnp.sqrt(jnp.sum(taps * taps, axis=1, keepdims=True))
        high = taps.astype(BF16)
        rows = pl.ds((8 + i) * GTAPS, GTAPS)
        box_gauss[rows, 0:LANES] = high
        box_gauss[rows, LANES : 2 * LANES] = high
        gauss_rest[pl.ds(i * GTAPS, GTAPS), :] = (taps - high.astype(F32)).astype(BF16)


def third_kernel(delays, widths, x, box_gauss, gauss_rest, plane, peaks, scratch):
    blocks = [x[v] for v in range(16)]
    for bit in range(4):

        def delay_of(v, bit=bit):
            row = block_row(v, bit + 1)
            return Delay(delays[bit, row], delays[bit, row + (2 << bit)])

        blocks = merge_blocks(blocks, bit, delay_of)
    for v in range(16):
        place = (v & 1) * 8 + block_row(v >> 1, 3)
        scratch[8 * place : 8 * place + 8, :] = blocks[v]
    halves = [[], []]
    for beam in range(2):
        for tile in range(4):
            for half in range(2):
                rows = scratch[
                    pl.ds((tile & 1) * 64 + (tile >> 1) * 4 + half * 2 + beam, 8, stride=8), :
                ]
                plane[beam, 8 * tile : 8 * tile + 8, half * LANES : (half + 1) * LANES] = rows
                halves[half].append(rows)
    first = jnp.concatenate(halves[0], axis=0)
    second = jnp.concatenate(halves[1], axis=0)
    early = lax.broadcasted_iota(jnp.int32, first.shape, 1) < GTAPS
    turned = pltpu.roll(second, GTAPS, 1)
    windows = jnp.concatenate(
        [
            first,
            jnp.where(early, pltpu.roll(first, GTAPS, 1), turned),
            second,
            jnp.where(early, turned, jnp.zeros_like(turned)),
        ],
        axis=0,
    )
    high = windows.astype(BF16)
    rest = (windows - high.astype(F32)).astype(BF16)
    both = jnp.concatenate([high, rest], axis=1)
    over = (((1,), (1,)), ((), ()))
    main = lax.dot_general(box_gauss[...], both, over, preferred_element_type=F32)
    small = lax.dot_general(gauss_rest[...], high, over, preferred_element_type=F32)
    best = []
    for i in range(16):
        value = main[i * GTAPS : (i + 1) * GTAPS]
        if i >= 8:
            value = value + small[(i - 8) * GTAPS : (i - 7) * GTAPS]
        value = jnp.maximum(value[:, :LANES], value[:, LANES:])
        value = jnp.max(value, axis=0, keepdims=True)
        if i < 8:
            value = value / jnp.sqrt(jnp.full(value.shape, widths[i], jnp.int32).astype(F32))
        best.append(value)
    best = jnp.concatenate(best, axis=0)
    best = jnp.maximum(best, pltpu.roll(best, GTAPS, 1))
    peaks[0] = best[:, :32]
    peaks[1] = pltpu.roll(best, LANES - 32, 1)[:, :32]


def whole(space=VMEM):
    return pl.BlockSpec(memory_space=space)


def shape_of(*dims, dtype=F32):
    return jax.ShapeDtypeStruct(dims, dtype)


def on_device(intensity, shift_table, box_widths):
    beams, channels, length = intensity.shape
    scale = float(channels * lax.axis_size(("z", "x", "beam"))) ** -0.5
    corner = pl.BlockSpec((8, LANES), lambda i: (0, 0), memory_space=SMEM)
    rows = pl.pallas_call(
        functools.partial(first_kernel, scale),
        grid=(1,),
        in_specs=[corner, pl.BlockSpec((beams * channels, length), lambda i: (0, 0))],
        out_specs=pl.BlockSpec((32, 4, LANES), lambda i: (0, 0, 0)),
        out_shape=shape_of(32, 4, LANES),
        scratch_shapes=[VMEM((2, beams * channels, LANES), F32)],
        name="channels_to_level_2",
    )(shift_table, intensity.reshape(beams * channels, length))
    rows = lax.all_to_all(rows, ("x", "beam"), split_axis=0, concat_axis=0, tiled=True)
    delays, box_gauss, gauss_rest = pl.pallas_call(
        prepare_kernel,
        in_specs=[whole(), whole(SMEM)],
        out_specs=[whole(), whole(), whole()],
        out_shape=[
            shape_of(4, LANES, dtype=jnp.int32),
            shape_of(16 * GTAPS, 2 * LANES, dtype=BF16),
            shape_of(8 * GTAPS, LANES, dtype=BF16),
        ],
        name="delays_and_taps",
    )(shift_table, box_widths)
    rows = pl.pallas_call(
        second_kernel,
        grid=(1,),
        in_specs=[corner, pl.BlockSpec((16, 8, LANES), lambda i: (0, 0, 0))],
        out_specs=pl.BlockSpec((16, 8, LANES), lambda i: (0, 0, 0)),
        out_shape=shape_of(16, 8, LANES),
        name="levels_3_to_7",
    )(shift_table, rows.reshape(16, 8, LANES))
    rows = lax.all_to_all(rows, "z", split_axis=0, concat_axis=0, tiled=True)
    return pl.pallas_call(
        third_kernel,
        in_specs=[whole(SMEM), whole(SMEM), whole(), whole(), whole()],
        out_specs=[whole(), whole()],
        out_shape=[shape_of(2, 32, length), shape_of(2, 16, 32)],
        scratch_shapes=[VMEM((LANES, LANES), F32)],
        name="levels_8_to_11_and_filters",
    )(delays, box_widths, rows, box_gauss, gauss_rest)


def solution(mesh):
    cube = Mesh(mesh.devices.reshape(16, 4, 8), ("z", "x", "beam"))
    in_specs = (P(None, ("z", "x", "beam"), None), P(), P())
    out_specs = (P("beam", ("z", "x"), None), P("beam", None, ("z", "x")))
    return jax.shard_map(
        on_device, mesh=cube, in_specs=in_specs, out_specs=out_specs, check_vma=False
    )
```

time: 91.7 us -> 50.5 us (0.55)
  the two profiles are of different devices: /device:TPU:8 before, /device:TPU:1 now
where the time goes in v1:
time: 50.5 us; the launch traced here: 50.2 us
  blocking collectives  18.5 us (37%)
  starting transfers between devices  12.5 us (25%)
  waiting for transfers between devices  9.57 us (19%)
  Pallas kernels  8.4 us (17%)
  between operations  0.64 us (1%)
  local copies, waits for them, and re-layouts  0.62 us (1%)
    all_to_all x1, blocking collectives, on_device(): lax.all_to_all(rows, ('x', 'beam'), split_axis=0, concat_axis=0, tiled=True)  18.5 us
    all_to_all x1, starting transfers between devices, on_device(): rows = lax.all_to_all(rows, 'z', split_axis=0, concat_axis=0, tiled=True)  12.5 us
    all_to_all x1, waiting for transfers between devices, on_device(): rows = lax.all_to_all(rows, 'z', split_axis=0, concat_axis=0, tiled=True)  9.57 us
    pallas_call x1, Pallas kernels, on_device(): pl.pallas_call(third_kernel, in_specs=[whole(SMEM), whole(SMEM), whole(),...  2.66 us
    pallas_call x1, Pallas kernels, on_device(): pl.pallas_call(prepare_kernel, in_specs=[whole(), whole(SMEM)], out_specs...  2.03 us
    pallas_call x1, Pallas kernels, on_device(): pl.pallas_call(second_kernel, grid=(1,), in_specs=[corner, pl.BlockSpec((...  1.91 us
    pallas_call x1, Pallas kernels, on_device(): pl.pallas_call(functools.partial(first_kernel, scale), grid=(1,), in_spec...  1.8 us
  transfers between devices with their start and end apart: 1, of which 1 were waited for; matrix products, arithmetic and copies ran while one was open for 0% of the time, Pallas kernels for 4%

profile of v1, /device:TPU:1, one launch (start us, length us, event | category | flops | bytes accessed | tf_op | source)
XLA Modules:
  0.0 50.2 jit_solution(8446037224423973973)
XLA Ops:
  0.6 1.8 %channels_to_level_2.1 = f32[32,4,128]{2,1,0:T(4,128)} custom-call(s32[11,2048]{1,0:T(8,128)} %table.5, f32[256,256]{1,0:T(8,128)} %bitcast.2), custom_call_target="tpu_custom_call" | custom-call | tf_op jit(solution)/shard_map/channels_to_level_2/pallas_call | solution.py:234
  2.4 18.5 %all_to_all.10 = f32[32,4,128]{2,1,0:T(4,128)} all-to-all(f32[32,4,128]{2,1,0:T(4,128)} %channels_to_level_2.1), channel_id=1, replica_groups=mesh['z'=16,'x'=4,'beam'=8] {'x','beam'}, dimensions={0} | all-to-all | bytes 131072 | tf_op jit(solution)/shard_map/all_to_all | solution.py:243
  20.9 1.9 %levels_3_to_7.1 = f32[16,8,128]{2,1,0:T(8,128)} custom-call(s32[11,2048]{1,0:T(8,128)} %table.5, f32[16,8,128]{2,1,0:T(8,128)} %bitcast.3), custom_call_target="tpu_custom_call" | custom-call | tf_op jit(solution)/shard_map/levels_3_to_7/pallas_call | solution.py:255
  22.9 12.5 %all-to-all-start.1 = ((f32[16,8,128]{2,1,0:T(8,128)}), f32[16,8,128]{2,1,0:T(8,128)S(1)}, u32[]{:S(2)}, u32[]{:S(2)}) async-start(f32[16,8,128]{2,1,0:T(8,128)} %levels_3_to_7.1), calls=%async_computation.1 | async-start | bytes 131072 | tf_op jit(solution)/shard_map/all_to_all | solution.py:263
  35.3 2.0 %delays_and_taps.1 = (s32[4,128]{1,0:T(4,128)}, bf16[1024,256]{1,0:T(8,128)(2,1)}, bf16[512,128]{1,0:T(8,128)(2,1)}) custom-call(s32[11,2048]{1,0:T(8,128)} %table.5, s32[8]{0:T(128)} %widths.3), custom_call_target="tpu_custom_call" | custom-call | tf_op jit(solution)/shard_map/delays_and_taps/pallas_call | solution.py:244
  37.3 9.6 %all-to-all-done.1.x = f32[16,8,128]{2,1,0:T(8,128)S(1)} async-done(((f32[16,8,128]{2,1,0:T(8,128)}), f32[16,8,128]{2,1,0:T(8,128)S(1)}, u32[]{:S(2)}, u32[]{:S(2)}) %all-to-all-start.1) | async-done | bytes 65568 | tf_op jit(solution)/shard_map/all_to_all | solution.py:263
  46.9 0.0 copy-start
  46.9 0.6 %copy-done = f32[16,8,128]{2,1,0:T(8,128)} copy-done((f32[16,8,128]{2,1,0:T(8,128)}, f32[16,8,128]{2,1,0:T(8,128)S(1)}, u32[]{:S(2)}) %copy-start) | copy-done | bytes 65560
  47.5 2.7 %levels_8_to_11_and_filters.1 = (f32[2,32,256]{2,1,0:T(8,128)}, f32[2,16,32]{2,1,0:T(8,128)}) custom-call(s32[4,128]{1,0:T(4,128)} %get-tuple-element.5.delays, s32[8]{0:T(128)} %widths.3, f32[16,8,128]{2,1,0:T(8,128)} %copy-done, bf16[1024,256]{1,0:T(8,128)(2,1)} %get-tuple-element.6.box_gauss, bf16[512,128]{1,0:T(8,128)(2,1)} %get-tuple-element.7.gauss_rest), custom_call_target="tpu_custom_call" | custom-call | tf_op jit(solution)/shard_map/levels_8_to_11_and_filters/pallas_call | solution.py:264
Async XLA Ops:
  22.9 24.1 %all-to-all-start.1 = ((f32[16,8,128]{2,1,0:T(8,128)}), f32[16,8,128]{2,1,0:T(8,128)S(1)}, u32[]{:S(2)}, u32[]{:S(2)}) async-start(f32[16,8,128]{2,1,0:T(8,128)} %levels_3_to_7.1), calls=%async_computation.1 | async-start | bytes 131072 | tf_op jit(solution)/shard_map/all_to_all | solution.py:263
  46.9 0.6 %copy-start = (f32[16,8,128]{2,1,0:T(8,128)}, f32[16,8,128]{2,1,0:T(8,128)S(1)}, u32[]{:S(2)}) copy-start(f32[16,8,128]{2,1,0:T(8,128)S(1)} %all-to-all-done.1.x) | copy-start | bytes 196612

commit v2 on v1

--- a/solution.py
+++ b/solution.py
@@ -11,6 +11,8 @@
 LANES = 128
 F32 = jnp.float32
 BF16 = jnp.bfloat16
+PLANE_FIRST = 20
+LINE_FIRST = 8
 SMEM = pltpu.SMEM
 VMEM = pltpu.VMEM
 LANEWISE = lax.GatherDimensionNumbers(
@@ -81,7 +83,7 @@
             row = merge_pair(pairs[0][d >> 1], pairs[1][d >> 1], table[1, d])
             for half in range(2):
                 for j in range(4):
-                    out[target * 8 + tile * 4 + j, 2 * half : 2 * half + 2, :] = row[half][
+                    out[(target * 8 + tile * 4 + j) ^ PLANE_FIRST, 2 * half : 2 * half + 2, :] = row[half][
                         2 * j : 2 * j + 2, :
                     ]
 
@@ -121,7 +123,7 @@
     delay = Delay(table[2, top * 2], table[2, top * 2 + 1])
     blocks = []
     for v in range(16):
-        a = x[v]
+        a = x[v ^ PLANE_FIRST // 2]
         b = pltpu.roll(a, 4, 0)
         blocks.append(jnp.where(low, a, b) + delay(jnp.where(low, b, a)))
     for bit in range(4):
@@ -134,8 +136,8 @@
         blocks = merge_blocks(blocks, bit, delay_of)
     for w in range(8):
         a, b = blocks[w], blocks[8 + w]
-        out[2 * w] = jnp.where(low, a, pltpu.roll(b, 4, 0))
-        out[2 * w + 1] = jnp.where(low, pltpu.roll(a, 4, 0), b)
+        out[2 * w ^ LINE_FIRST] = jnp.where(low, a, pltpu.roll(b, 4, 0))
+        out[2 * w + 1 ^ LINE_FIRST] = jnp.where(low, pltpu.roll(a, 4, 0), b)
 
 
 def prepare_kernel(table, widths, delays, box_gauss, gauss_rest):
@@ -164,7 +166,7 @@
 
 
 def third_kernel(delays, widths, x, box_gauss, gauss_rest, plane, peaks, scratch):
-    blocks = [x[v] for v in range(16)]
+    blocks = [x[v ^ LINE_FIRST] for v in range(16)]
     for bit in range(4):
 
         def delay_of(v, bit=bit):
@@ -219,6 +221,13 @@
     peaks[1] = pltpu.roll(best, LANES - 32, 1)[:, :32]
 
 
+def exchanged(rows, axis, first):
+    members = [place ^ first for place in range(lax.axis_size(axis))]
+    return lax.all_to_all(
+        rows, axis, split_axis=0, concat_axis=0, tiled=True, axis_index_groups=[members]
+    )
+
+
 def whole(space=VMEM):
     return pl.BlockSpec(memory_space=space)
 
@@ -238,9 +247,10 @@
         out_specs=pl.BlockSpec((32, 4, LANES), lambda i: (0, 0, 0)),
         out_shape=shape_of(32, 4, LANES),
         scratch_shapes=[VMEM((2, beams * channels, LANES), F32)],
+        compiler_params=pltpu.CompilerParams(vmem_limit_bytes=8 << 20),
         name="channels_to_level_2",
     )(shift_table, intensity.reshape(beams * channels, length))
-    rows = lax.all_to_all(rows, ("x", "beam"), split_axis=0, concat_axis=0, tiled=True)
+    rows = exchanged(rows, ("x", "beam"), PLANE_FIRST)
     delays, box_gauss, gauss_rest = pl.pallas_call(
         prepare_kernel,
         in_specs=[whole(), whole(SMEM)],
@@ -250,6 +260,7 @@
             shape_of(16 * GTAPS, 2 * LANES, dtype=BF16),
             shape_of(8 * GTAPS, LANES, dtype=BF16),
         ],
+        compiler_params=pltpu.CompilerParams(vmem_limit_bytes=8 << 20),
         name="delays_and_taps",
     )(shift_table, box_widths)
     rows = pl.pallas_call(
@@ -258,15 +269,17 @@
         in_specs=[corner, pl.BlockSpec((16, 8, LANES), lambda i: (0, 0, 0))],
         out_specs=pl.BlockSpec((16, 8, LANES), lambda i: (0, 0, 0)),
         out_shape=shape_of(16, 8, LANES),
+        compiler_params=pltpu.CompilerParams(vmem_limit_bytes=8 << 20),
         name="levels_3_to_7",
     )(shift_table, rows.reshape(16, 8, LANES))
-    rows = lax.all_to_all(rows, "z", split_axis=0, concat_axis=0, tiled=True)
+    rows = exchanged(rows, "z", LINE_FIRST)
     return pl.pallas_call(
         third_kernel,
         in_specs=[whole(SMEM), whole(SMEM), whole(), whole(), whole()],
         out_specs=[whole(), whole()],
         out_shape=[shape_of(2, 32, length), shape_of(2, 16, 32)],
         scratch_shapes=[VMEM((LANES, LANES), F32)],
+        compiler_params=pltpu.CompilerParams(vmem_limit_bytes=8 << 20),
         name="levels_8_to_11_and_filters",
     )(delays, box_widths, rows, box_gauss, gauss_rest)
 

time: 50.5 us -> 42 us (0.83)
  waiting for transfers between devices: 9.57 us -> 3.07 us
  Pallas kernels: 8.4 us -> 5.42 us
  blocking collectives: 18.5 us -> 16 us
  starting transfers between devices: 12.5 us -> 14.7 us
  local copies, waits for them, and re-layouts: 0.62 us -> 1.86 us
    all_to_all x1, waiting for transfers between devices: 9.57 us -> 3.07 us  [exchanged(): lax.all_to_all(rows, axis, split_axis=0, concat_axis=0, tiled=True, axis_...]
    all_to_all x1, blocking collectives: 18.5 us -> 16 us  [exchanged(): lax.all_to_all(rows, axis, split_axis=0, concat_axis=0, tiled=True, axis_...]
    all_to_all x1, starting transfers between devices: 12.5 us -> 14.7 us  [exchanged(): lax.all_to_all(rows, axis, split_axis=0, concat_axis=0, tiled=True, axis_...]
    unnamed x2 -> x8, local copies, waits for them, and re-layouts: 0.62 us -> 1.86 us
    pallas_call x1, Pallas kernels: 2.03 us -> 0.82 us  [on_device(): pl.pallas_call(prepare_kernel, in_specs=[whole(), whole(SMEM)], out_specs...]
    pallas_call x1, Pallas kernels: 1.8 us -> 0.8 us  [on_device(): pl.pallas_call(functools.partial(first_kernel, scale), grid=(1,), in_spec...]
    pallas_call x1, Pallas kernels: 2.66 us -> 2.14 us  [on_device(): pl.pallas_call(third_kernel, in_specs=[whole(SMEM), whole(SMEM), whole(),...]
  transfers between devices with their start and end apart: 1 -> 1, of which waited for: 1 -> 1; matrix products, arithmetic and copies ran while one was open for 0% -> 0% of each run, Pallas kernels for 4% -> 2%
where the time goes in v2:
time: 42 us; the launch traced here: 41.7 us
  blocking collectives  16 us (38%)
  starting transfers between devices  14.7 us (35%)
  Pallas kernels  5.42 us (13%)
  waiting for transfers between devices  3.07 us (7%)
  local copies, waits for them, and re-layouts  1.86 us (4%)
  between operations  0.66 us (2%)
    all_to_all x1, blocking collectives, exchanged(): lax.all_to_all(rows, axis, split_axis=0, concat_axis=0, tiled=True, axis_...  16 us
    all_to_all x1, starting transfers between devices, exchanged(): lax.all_to_all(rows, axis, split_axis=0, concat_axis=0, tiled=True, axis_...  14.7 us
    all_to_all x1, waiting for transfers between devices, exchanged(): lax.all_to_all(rows, axis, split_axis=0, concat_axis=0, tiled=True, axis_...  3.07 us
    pallas_call x1, Pallas kernels, on_device(): pl.pallas_call(third_kernel, in_specs=[whole(SMEM), whole(SMEM), whole(),...  2.14 us
    unnamed x8, local copies, waits for them, and re-layouts  1.86 us
    pallas_call x1, Pallas kernels, on_device(): pl.pallas_call(second_kernel, grid=(1,), in_specs=[corner, pl.BlockSpec((...  1.66 us
  transfers between devices with their start and end apart: 1, of which 1 were waited for; matrix products, arithmetic and copies ran while one was open for 0% of the time, Pallas kernels for 2%

profile of v2, /device:TPU:1, one launch (start us, length us, event | category | flops | bytes accessed | tf_op | source)
XLA Modules:
  0.0 41.7 jit_solution(13407133964980238346)
XLA Ops:
  0.6 0.0 copy-start
  0.6 0.9 %copy-done = s32[11,2048]{1,0:T(8,128)S(1)} copy-done((s32[11,2048]{1,0:T(8,128)S(1)}, s32[11,2048]{1,0:T(8,128)}, u32[]{:S(2)}) %copy-start) | copy-done | bytes 90136
  1.5 0.0 copy-start.2
  1.5 0.9 %copy-done.2 = f32[16,16,256]{2,1,0:T(8,128)S(1)} copy-done((f32[16,16,256]{2,1,0:T(8,128)S(1)}, f32[16,16,256]{2,1,0:T(8,128)}, u32[]{:S(2)}) %copy-start.2) | copy-done | bytes 262168
  2.5 0.8 %channels_to_level_2.1 = f32[32,4,128]{2,1,0:T(4,128)S(1)} custom-call(s32[11,2048]{1,0:T(8,128)S(1)} %copy-done, f32[256,256]{1,0:T(8,128)S(1)} %bitcast.2), custom_call_target="tpu_custom_call" | custom-call | tf_op jit(solution)/shard_map/channels_to_level_2/pallas_call | solution.py:243
  3.3 16.0 %all_to_all.10 = f32[32,4,128]{2,1,0:T(4,128)S(1)} all-to-all(f32[32,4,128]{2,1,0:T(4,128)S(1)} %channels_to_level_2.1), channel_id=1, replica_groups={{20,21,22,23,16,17,18,19,28,29,30,31,24,25,26,27,4,5,6,7,0,1,2,3,12,13,..., dimensions={0} | all-to-all | bytes 131072 | tf_op jit(solution)/shard_map/all_to_all | solution.py:226
  19.3 0.0 copy-start.3
  19.3 1.7 %levels_3_to_7.1 = f32[16,8,128]{2,1,0:T(8,128)} custom-call(s32[11,2048]{1,0:T(8,128)S(1)} %copy-done, f32[16,8,128]{2,1,0:T(8,128)S(1)} %bitcast.3), custom_call_target="tpu_custom_call" | custom-call | tf_op jit(solution)/shard_map/levels_3_to_7/pallas_call | solution.py:266
  21.0 0.0 copy-start.1
  21.0 14.7 %all-to-all-start.1 = ((f32[16,8,128]{2,1,0:T(8,128)}), f32[16,8,128]{2,1,0:T(8,128)S(1)}, u32[]{:S(2)}, u32[]{:S(2)}) async-start(f32[16,8,128]{2,1,0:T(8,128)} %levels_3_to_7.1), calls=%async_computation.1 | async-start | bytes 131072 | tf_op jit(solution)/shard_map/all_to_all | solution.py:226
  35.7 0.0 copy-done.3
  35.7 0.0 copy-done.1
  35.7 0.8 %delays_and_taps.1 = (s32[4,128]{1,0:T(4,128)S(1)}, bf16[1024,256]{1,0:T(8,128)(2,1)S(1)}, bf16[512,128]{1,0:T(8,128)(2,1)S(1)}) custom-call(s32[11,2048]{1,0:T(8,128)S(1)} %copy-done.1, s32[8]{0:T(128)S(1)} %copy-done.3), custom_call_target="tpu_custom_call" | custom-call | tf_op jit(solution)/shard_map/delays_and_taps/pallas_call | solution.py:254
  36.5 3.1 %all-to-all-done.1.x = f32[16,8,128]{2,1,0:T(8,128)S(1)} async-done(((f32[16,8,128]{2,1,0:T(8,128)}), f32[16,8,128]{2,1,0:T(8,128)S(1)}, u32[]{:S(2)}, u32[]{:S(2)}) %all-to-all-start.1) | async-done | bytes 65568 | tf_op jit(solution)/shard_map/all_to_all | solution.py:226
  39.6 2.1 %levels_8_to_11_and_filters.1 = (f32[2,32,256]{2,1,0:T(8,128)}, f32[2,16,32]{2,1,0:T(8,128)}) custom-call(s32[4,128]{1,0:T(4,128)S(1)} %get-tuple-element.5.delays, s32[8]{0:T(128)S(1)} %copy-done.3, f32[16,8,128]{2,1,0:T(8,128)S(1)} %all-to-all-done.1.x, bf16[1024,256]{1,0:T(8,128)(2,1)S(1)} %get-tuple-element.6.box_gauss, ...), custom_call_target="tpu_custom_call" | custom-call | tf_op jit(solution)/shard_map/levels_8_to_11_and_filters/pallas_call | solution.py:276
Async XLA Ops:
  0.6 0.9 %copy-start = (s32[11,2048]{1,0:T(8,128)S(1)}, s32[11,2048]{1,0:T(8,128)}, u32[]{:S(2)}) copy-start(s32[11,2048]{1,0:T(8,128)} %table.5) | copy-start | bytes 270340
  1.5 0.9 %copy-start.2 = (f32[16,16,256]{2,1,0:T(8,128)S(1)}, f32[16,16,256]{2,1,0:T(8,128)}, u32[]{:S(2)}) copy-start(f32[16,16,256]{2,1,0:T(8,128)} %param.3) | copy-start | bytes 786436
  19.3 16.4 %copy-start.3 = (s32[8]{0:T(128)S(1)}, s32[8]{0:T(128)}, u32[]{:S(2)}) copy-start(s32[8]{0:T(128)} %widths.3) | copy-start | bytes 100
  21.0 14.7 %copy-start.1 = (s32[11,2048]{1,0:T(8,128)S(1)}, s32[11,2048]{1,0:T(8,128)}, u32[]{:S(2)}) copy-start(s32[11,2048]{1,0:T(8,128)} %table.5) | copy-start | bytes 270340
  21.0 18.6 %all-to-all-start.1 = ((f32[16,8,128]{2,1,0:T(8,128)}), f32[16,8,128]{2,1,0:T(8,128)S(1)}, u32[]{:S(2)}, u32[]{:S(2)}) async-start(f32[16,8,128]{2,1,0:T(8,128)} %levels_3_to_7.1), calls=%async_computation.1 | async-start | bytes 131072 | tf_op jit(solution)/shard_map/all_to_all | solution.py:226

commit v3 on v2

v3 whole, which is shorter than its diff:
```python
import functools

import jax
import jax.numpy as jnp
from jax import lax
from jax.experimental import pallas as pl
from jax.experimental.pallas import tpu as pltpu
from jax.sharding import Mesh, PartitionSpec as P

GTAPS = 64
LANES = 128
F32 = jnp.float32
BF16 = jnp.bfloat16
PLANE_FIRST = 20
LINE_FIRST = 8
SMEM = pltpu.SMEM
VMEM = pltpu.VMEM
HBM = pltpu.HBM
LANEWISE = lax.GatherDimensionNumbers(
    offset_dims=(),
    collapsed_slice_dims=(1,),
    start_index_map=(1,),
    operand_batching_dims=(0,),
    start_indices_batching_dims=(0,),
)


def pick(block, index):
    return lax.gather(
        block, index[..., None], LANEWISE, (1, 1), mode=lax.GatherScatterMode.PROMISE_IN_BOUNDS
    )


def reversed_bits(value, bits):
    result = 0
    for place in range(bits):
        result = result + (value // (1 << place)) % 2 * (1 << (bits - 1 - place))
    return result


def iota(axis):
    return lax.broadcasted_iota(jnp.int32, (8, LANES), axis)


def delayed_pair(first, second, delay):
    source = iota(1) + delay
    index = source & (LANES - 1)
    near = source < LANES
    a = pick(first, index)
    b = pick(second, index)
    zero = jnp.zeros_like(a)
    return (
        jnp.where(near, a, jnp.where(source < 2 * LANES, b, zero)),
        jnp.where(near, b, zero),
    )


def merge_pair(lower, upper, delay):
    moved = delayed_pair(*upper, delay)
    return lower[0] + moved[0], lower[1] + moved[1]


def spread(row, place):
    return jnp.broadcast_to(row[:, place : place + 1], (8, LANES))


def first_kernel(scale, table, x, out, corner, split, corner_done, split_done):
    tiles = x.shape[0] // 128
    corner_copy = pltpu.make_async_copy(
        table.at[pl.ds(0, 8), pl.ds(0, LANES)], corner, corner_done
    )
    corner_copy.start()
    copies = []
    for tile in range(tiles):
        for half in range(2):
            copy = pltpu.make_async_copy(
                x.at[pl.ds(tile * 128, 128), pl.ds(half * LANES, LANES)],
                split.at[tile, half],
                split_done.at[tile, half],
            )
            copy.start()
            copies.append(copy)
    corner_copy.wait()
    first_delays = [spread(corner[0:1, :], d) for d in range(2)]
    second_delays = [spread(corner[1:2, :], d) for d in range(4)]
    for tile in range(tiles):
        copies[2 * tile].wait()
        copies[2 * tile + 1].wait()
        subbands = []
        for s in range(4):
            halves = []
            for half in range(2):
                parts = [split[tile, half, pl.ds(4 * s + c, 8, stride=16), :] for c in range(4)]
                halves.append(((parts[0] + parts[1]) + (parts[2] + parts[3])) * scale)
            subbands.append(tuple(halves))
        pairs = [
            [merge_pair(subbands[2 * g], subbands[2 * g + 1], first_delays[d]) for d in range(2)]
            for g in range(2)
        ]
        for target in range(4):
            d = (target & 1) * 2 + (target >> 1)
            row = merge_pair(pairs[0][d >> 1], pairs[1][d >> 1], second_delays[d])
            for half in range(2):
                for j in range(4):
                    place = (target * 8 + tile * 4 + j) ^ PLANE_FIRST
                    out[place, 2 * half : 2 * half + 2, :] = row[half][2 * j : 2 * j + 2, :]


def delayed(block, delay):
    source = iota(1) + delay
    a = pick(block, source & (LANES - 1))
    other = pltpu.roll(a, 6, 0)
    follows = (source < 2 * LANES) & ((iota(0) & 2) == 0)
    return jnp.where(source < LANES, a, jnp.where(follows, other, jnp.zeros_like(a)))


def merge_blocks(blocks, bit, delays, start):
    return [
        blocks[v & ~(1 << bit)]
        + delayed(blocks[v | 1 << bit], delays[start + (v & ((2 << bit) - 1))])
        for v in range(len(blocks))
    ]


def block_row(v, bits):
    return sum((v >> m & 1) << (bits - 1 - m) for m in range(bits))


def second_kernel(delays, x, out):
    low = iota(0) < 4
    blocks = []
    for v in range(16):
        a = x[v ^ PLANE_FIRST // 2]
        b = pltpu.roll(a, 4, 0)
        blocks.append(jnp.where(low, a, b) + delayed(jnp.where(low, b, a), delays[0]))
    for bit in range(4):
        blocks = merge_blocks(blocks, bit, delays, (2 << bit) - 1)
    for w in range(8):
        a, b = blocks[w], blocks[8 + w]
        out[2 * w ^ LINE_FIRST] = jnp.where(low, a, pltpu.roll(b, 4, 0))
        out[2 * w + 1 ^ LINE_FIRST] = jnp.where(low, pltpu.roll(a, 4, 0), b)


def prepare_kernel(table, widths, second, third, box_gauss, gauss_rest, box_scale):
    top = reversed_bits(lax.axis_index("x"), 2)
    block = top * 16 + reversed_bits(lax.axis_index("z"), 4)
    low = iota(0) < 4

    def level_row(level, base):
        row = table[level : level + 1, pl.ds(pl.multiple_of(base // LANES * LANES, LANES), LANES)]
        return pltpu.roll(row, (LANES - base % LANES) % LANES, 1)

    row = level_row(2, top * 2)
    second[0] = jnp.where(low, spread(row, 0), spread(row, 1))
    for bit in range(4):
        kinds = 2 << bit
        for out, row, start in (
            (second, level_row(3 + bit, top * 2 * kinds), kinds - 1),
            (third, level_row(7 + bit, block * 2 * kinds), kinds - 2),
        ):
            for v in range(kinds):
                d = block_row(v, bit + 1)
                out[start + v] = jnp.where(low, spread(row, d), spread(row, d + kinds))
    shape = (GTAPS, LANES)
    lag = lax.broadcasted_iota(jnp.int32, shape, 1) - lax.broadcasted_iota(jnp.int32, shape, 0)
    valid = (lag >= 0) & (lag < GTAPS)
    offset = lag.astype(F32) - float(GTAPS // 2)
    for i in range(8):
        rows = pl.ds(i * GTAPS, GTAPS)
        ones = jnp.where((lag >= 0) & (lag < widths[i]), 1.0, 0.0).astype(BF16)
        box_gauss[rows, 0:LANES] = ones
        box_gauss[rows, LANES : 2 * LANES] = ones
        width = jnp.full(shape, widths[i], jnp.int32).astype(F32)
        box_scale[i : i + 1, :] = jnp.sqrt(width[0:1, :])
        sigma = width / 2.3548
        taps = jnp.where(valid, jnp.exp(-0.5 * (offset / sigma) ** 2), 0.0)
        taps = taps / jnp.sqrt(jnp.sum(taps * taps, axis=1, keepdims=True))
        high = taps.astype(BF16)
        rows = pl.ds((8 + i) * GTAPS, GTAPS)
        box_gauss[rows, 0:LANES] = high
        box_gauss[rows, LANES : 2 * LANES] = high
        gauss_rest[pl.ds(i * GTAPS, GTAPS), :] = (taps - high.astype(F32)).astype(BF16)


def third_kernel(
    delays, box_scale, x, box_gauss, gauss_rest, plane, peaks, scratch, held, plane_done
):
    blocks = [x[v ^ LINE_FIRST] for v in range(16)]
    for bit in range(4):
        blocks = merge_blocks(blocks, bit, delays, (2 << bit) - 2)
    for v in range(16):
        place = (v & 1) * 8 + block_row(v >> 1, 3)
        scratch[8 * place : 8 * place + 8, :] = blocks[v]
    halves = [[], []]
    for beam in range(2):
        for tile in range(4):
            for half in range(2):
                rows = scratch[
                    pl.ds((tile & 1) * 64 + (tile >> 1) * 4 + half * 2 + beam, 8, stride=8), :
                ]
                held[beam, 8 * tile : 8 * tile + 8, half * LANES : (half + 1) * LANES] = rows
                halves[half].append(rows)
    copy = pltpu.make_async_copy(held, plane, plane_done)
    copy.start()
    first = jnp.concatenate(halves[0], axis=0)
    second = jnp.concatenate(halves[1], axis=0)
    early = lax.broadcasted_iota(jnp.int32, first.shape, 1) < GTAPS
    turned = pltpu.roll(second, GTAPS, 1)
    windows = jnp.concatenate(
        [
            first,
            jnp.where(early, pltpu.roll(first, GTAPS, 1), turned),
            second,
            jnp.where(early, turned, jnp.zeros_like(turned)),
        ],
        axis=0,
    )
    high = windows.astype(BF16)
    rest = (windows - high.astype(F32)).astype(BF16)
    both = jnp.concatenate([high, rest], axis=1)
    over = (((1,), (1,)), ((), ()))
    main = lax.dot_general(box_gauss[...], both, over, preferred_element_type=F32)
    small = lax.dot_general(gauss_rest[...], high, over, preferred_element_type=F32)
    best = []
    for i in range(16):
        value = main[i * GTAPS : (i + 1) * GTAPS]
        if i >= 8:
            value = value + small[(i - 8) * GTAPS : (i - 7) * GTAPS]
        value = jnp.maximum(value[:, :LANES], value[:, LANES:])
        value = jnp.max(value, axis=0, keepdims=True)
        best.append(value)
    best = jnp.concatenate(
        [jnp.concatenate(best[:8], axis=0) / box_scale[...], jnp.concatenate(best[8:], axis=0)],
        axis=0,
    )
    best = jnp.maximum(best, pltpu.roll(best, GTAPS, 1))
    peaks[0] = best[:, :32]
    peaks[1] = pltpu.roll(best, LANES - 32, 1)[:, :32]
    copy.wait()


def exchanged(rows, axis, first):
    members = [place ^ first for place in range(lax.axis_size(axis))]
    return lax.all_to_all(
        rows, axis, split_axis=0, concat_axis=0, tiled=True, axis_index_groups=[members]
    )


def whole(space=VMEM):
    return pl.BlockSpec(memory_space=space)


def shape_of(*dims, dtype=F32):
    return jax.ShapeDtypeStruct(dims, dtype)


def kernel_call(body, name, ins, outs, shapes, scratch=(), room=8):
    return pl.pallas_call(
        body,
        in_specs=[whole(space) for space in ins],
        out_specs=[whole(space) for space in outs],
        out_shape=shapes,
        scratch_shapes=list(scratch),
        compiler_params=pltpu.CompilerParams(vmem_limit_bytes=room << 20),
        name=name,
    )


def on_device(intensity, shift_table, box_widths):
    beams, channels, length = intensity.shape
    scale = float(channels * lax.axis_size(("z", "x", "beam"))) ** -0.5
    [rows] = kernel_call(
        functools.partial(first_kernel, scale),
        "channels_to_level_2",
        [HBM, HBM],
        [VMEM],
        [shape_of(32, 4, LANES)],
        [
            VMEM((8, LANES), jnp.int32),
            VMEM((beams // 8, 2, LANES, LANES), F32),
            pltpu.SemaphoreType.DMA,
            pltpu.SemaphoreType.DMA((beams // 8, 2)),
        ],
        room=60,
    )(shift_table, intensity.reshape(beams * channels, length))
    rows = exchanged(rows, ("x", "beam"), PLANE_FIRST)
    second, third, box_gauss, gauss_rest, box_scale = kernel_call(
        prepare_kernel,
        "delays_and_taps",
        [VMEM, SMEM],
        [VMEM] * 5,
        [
            shape_of(31, 8, LANES, dtype=jnp.int32),
            shape_of(30, 8, LANES, dtype=jnp.int32),
            shape_of(16 * GTAPS, 2 * LANES, dtype=BF16),
            shape_of(8 * GTAPS, LANES, dtype=BF16),
            shape_of(8, LANES),
        ],
    )(shift_table, box_widths)
    [rows] = kernel_call(
        second_kernel, "levels_3_to_7", [VMEM, VMEM], [VMEM], [shape_of(16, 8, LANES)]
    )(second, rows.reshape(16, 8, LANES))
    rows = exchanged(rows, "z", LINE_FIRST)
    return tuple(
        kernel_call(
            third_kernel,
            "levels_8_to_11_and_filters",
            [VMEM] * 5,
            [pl.ANY, VMEM],
            [shape_of(2, 32, length), shape_of(2, 16, 32)],
            [
                VMEM((LANES, LANES), F32),
                VMEM((2, 32, length), F32),
                pltpu.SemaphoreType.DMA,
            ],
        )(third, box_scale, rows, box_gauss, gauss_rest)
    )


def solution(mesh):
    cube = Mesh(mesh.devices.reshape(16, 4, 8), ("z", "x", "beam"))
    in_specs = (P(None, ("z", "x", "beam"), None), P(), P())
    out_specs = (P("beam", ("z", "x"), None), P("beam", None, ("z", "x")))
    return jax.shard_map(
        on_device, mesh=cube, in_specs=in_specs, out_specs=out_specs, check_vma=False
    )
```

time: 42 us -> 39.7 us (0.945)
  blocking collectives: 16 us -> 18.5 us
  local copies, waits for them, and re-layouts: 1.86 us -> 0.01 us
  waiting for transfers between devices: 3.07 us -> 1.26 us
  starting transfers between devices: 14.7 us -> 14 us
  Pallas kernels: 5.42 us -> 4.94 us
    all_to_all x1, blocking collectives: 16 us -> 18.5 us  [exchanged(): lax.all_to_all(rows, axis, split_axis=0, concat_axis=0, tiled=True, axis_...]
    unnamed x8 -> x4, local copies, waits for them, and re-layouts: 1.86 us -> 0.01 us
    all_to_all x1, waiting for transfers between devices: 3.07 us -> 1.26 us  [exchanged(): lax.all_to_all(rows, axis, split_axis=0, concat_axis=0, tiled=True, axis_...]
    all_to_all x1, starting transfers between devices: 14.7 us -> 14 us  [exchanged(): lax.all_to_all(rows, axis, split_axis=0, concat_axis=0, tiled=True, axis_...]
    pallas_call x4, Pallas kernels: 5.42 us -> 4.94 us  [the longest x1 1.9 us: on_device(): kernel_call(functools.partial(first_kernel, scale), 'channels_to_level_2'...]
  transfers between devices with their start and end apart: 1 -> 1, of which waited for: 1 -> 1; matrix products, arithmetic and copies ran while one was open for 0% -> 0% of each run, Pallas kernels for 2% -> 3%
where the time goes in v3:
time: 39.7 us; the launch traced here: 39.5 us
  blocking collectives  18.5 us (47%)
  starting transfers between devices  14 us (35%)
  Pallas kernels  4.94 us (12%)
  waiting for transfers between devices  1.26 us (3%)
  between operations  0.69 us (2%)
    all_to_all x1, blocking collectives, exchanged(): lax.all_to_all(rows, axis, split_axis=0, concat_axis=0, tiled=True, axis_...  18.5 us
    all_to_all x1, starting transfers between devices, exchanged(): lax.all_to_all(rows, axis, split_axis=0, concat_axis=0, tiled=True, axis_...  14 us
    pallas_call x1, Pallas kernels, on_device(): kernel_call(functools.partial(first_kernel, scale), 'channels_to_level_2'...  1.9 us
    pallas_call x1, Pallas kernels, on_device(): kernel_call(third_kernel, 'levels_8_to_11_and_filters', [VMEM] * 5, [pl.A...  1.6 us
    all_to_all x1, waiting for transfers between devices, exchanged(): lax.all_to_all(rows, axis, split_axis=0, concat_axis=0, tiled=True, axis_...  1.26 us
    pallas_call x1, Pallas kernels, on_device(): kernel_call(prepare_kernel, 'delays_and_taps', [VMEM, SMEM], [VMEM] * 5,...  1.04 us
  transfers between devices with their start and end apart: 1, of which 1 were waited for; matrix products, arithmetic and copies ran while one was open for 0% of the time, Pallas kernels for 3%

profile of v3, /device:TPU:1, one launch (start us, length us, event | category | flops | bytes accessed | tf_op | source)
XLA Modules:
  0.0 39.5 jit_solution(8243585887397346969)
XLA Ops:
  0.6 0.0 copy-start.1
  0.6 1.9 %channels_to_level_2.1 = f32[32,4,128]{2,1,0:T(4,128)} custom-call(s32[11,2048]{1,0:T(8,128)} %table.3, f32[256,256]{1,0:T(8,128)} %bitcast.3), custom_call_target="tpu_custom_call" | custom-call | tf_op jit(solution)/shard_map/channels_to_level_2/pallas_call | solution.py:272
  2.5 0.0 copy-start
  2.6 14.0 %all-to-all-start = ((f32[32,4,128]{2,1,0:T(4,128)}), f32[32,4,128]{2,1,0:T(4,128)S(1)}, u32[]{:S(2)}, u32[]{:S(2)}) async-start(f32[32,4,128]{2,1,0:T(4,128)} %channels_to_level_2.1), calls=%async_computation | async-start | bytes 131072 | tf_op jit(solution)/shard_map/all_to_all | solution.py:244
  16.6 0.0 copy-done.1
  16.6 0.0 copy-done
  16.6 1.0 %delays_and_taps.1 = (s32[31,8,128]{2,1,0:T(8,128)S(1)}, s32[30,8,128]{2,1,0:T(8,128)S(1)}, bf16[1024,256]{1,0:T(8,128)(2,1)S(1)}, bf16[512,128]{1,0:T(8,128)(2,1)S(1)}, f32[8,128]{1,0:T(8,128)S(1)}) custom-call(s32[11,2048]{1,0:T(8,128)S(1)} %copy-done, s32[8]{0:T(128)S(1)} %copy-done.1), custom_call_target="tpu_custom_call" | custom-call | tf_op jit(solution)/shard_map/delays_and_taps/pallas_call | solution.py:287
  17.7 1.3 %all-to-all-done = f32[32,4,128]{2,1,0:T(4,128)S(1)} async-done(((f32[32,4,128]{2,1,0:T(4,128)}), f32[32,4,128]{2,1,0:T(4,128)S(1)}, u32[]{:S(2)}, u32[]{:S(2)}) %all-to-all-start) | async-done | bytes 65568 | tf_op jit(solution)/shard_map/all_to_all | solution.py:244
  18.9 0.4 %levels_3_to_7.1 = f32[16,8,128]{2,1,0:T(8,128)S(1)} custom-call(s32[31,8,128]{2,1,0:T(8,128)S(1)} %get-tuple-element.9.delays, f32[16,8,128]{2,1,0:T(8,128)S(1)} %bitcast.2), custom_call_target="tpu_custom_call" | custom-call | tf_op jit(solution)/shard_map/levels_3_to_7/pallas_call | solution.py:300
  19.3 18.5 %all_to_all.10.x = f32[16,8,128]{2,1,0:T(8,128)S(1)} all-to-all(f32[16,8,128]{2,1,0:T(8,128)S(1)} %levels_3_to_7.1), channel_id=1, replica_groups={{256,288,320,352,384,416,448,480,0,32,64,96,128,160,192,224},{257,289,3..., dimensions={0} | all-to-all | bytes 131072 | tf_op jit(solution)/shard_map/all_to_all | solution.py:244
  37.9 1.6 %levels_8_to_11_and_filters.1 = (f32[2,32,256]{2,1,0:T(8,128)}, f32[2,16,32]{2,1,0:T(8,128)}) custom-call(s32[30,8,128]{2,1,0:T(8,128)S(1)} %get-tuple-element.7.delays, f32[8,128]{1,0:T(8,128)S(1)} %get-tuple-element.8.box_scale, f32[16,8,128]{2,1,0:T(8,128)S(1)} %all_to_all.10.x, bf16[1024,256]{1,0:T(8,128)(2,1)S(1)} %get-tuple-element.10.box_gauss, ...), custom_call_target="tpu_custom_call" | custom-call | tf_op jit(solution)/shard_map/levels_8_to_11_and_filters/pallas_call | solution.py:305
Async XLA Ops:
  0.6 16.0 %copy-start.1 = (s32[8]{0:T(128)S(1)}, s32[8]{0:T(128)}, u32[]{:S(2)}) copy-start(s32[8]{0:T(128)} %widths.1) | copy-start | bytes 100
  2.5 14.1 %copy-start = (s32[11,2048]{1,0:T(8,128)S(1)}, s32[11,2048]{1,0:T(8,128)}, u32[]{:S(2)}) copy-start(s32[11,2048]{1,0:T(8,128)} %table.3) | copy-start | bytes 270340
  2.6 16.4 %all-to-all-start = ((f32[32,4,128]{2,1,0:T(4,128)}), f32[32,4,128]{2,1,0:T(4,128)S(1)}, u32[]{:S(2)}, u32[]{:S(2)}) async-start(f32[32,4,128]{2,1,0:T(4,128)} %channels_to_level_2.1), calls=%async_computation | async-start | bytes 131072 | tf_op jit(solution)/shard_map/all_to_all | solution.py:244
